TPU v7x, 32 devices: a whole 2x2x4 slice. The times are simulated.
32 devices in a mesh: dp: 2 (over x), cent: 16 (over z, y, core).
Axes of the slice: x: 2, y: 2, z: 4, core: 2. Of those that a mesh axis runs over, the one named last changes fastest.
Arguments:
- vectors: bfloat16 [512, 1024], P(('dp', 'cent')), may hold values from -16 to 16
- centroids: bfloat16 [65536, 1024], P('cent'), may hold values from -0.1125 to 0.1125
Outputs:
- new_centroids: bfloat16 [65536, 1024], P('cent', 'dp')
- loads: float32 [65536], P('cent')
All inputs are finite; a program needn't handle non-finite values.
Results may differ from a plain program's by a relative error of at most 0.0075.
Values may be sent and summed in bfloat16 or wider, within the bound.
A program may use at most 128 MiB of HBM per device.

v0:
```python
import jax
import jax.numpy as jnp
from jax import lax
from jax.sharding import PartitionSpec as P

softness_scale = 0.1


def on_device(vectors, centroids):
    dp = lax.axis_size("dp")
    cent = lax.axis_size("cent")
    total_rows = vectors.shape[0] * dp * cent
    mass_scale = centroids.shape[0] * cent / total_rows
    rows = lax.all_gather(vectors, ("dp", "cent"), axis=0, tiled=True)
    scores = (
        lax.dot_general(
            centroids, rows, (((1,), (1,)), ((), ())), preferred_element_type=jnp.float32
        )
        / softness_scale
    )
    local_peak = jnp.max(scores, axis=0)
    exponent = jnp.exp(scores - local_peak[None, :])
    local_sum = jnp.sum(exponent, axis=0)
    stats = lax.all_gather(jnp.stack([local_peak, local_sum]), "cent", axis=0)
    highest = jnp.max(stats[:, 0], axis=0)
    summed = jnp.sum(stats[:, 1] * jnp.exp(stats[:, 0] - highest[None, :]), axis=0)
    rescale = jnp.exp(local_peak - highest) / summed
    probability = exponent * rescale[None, :]
    weights = probability.astype(jnp.bfloat16)
    loads = jnp.sum(probability, axis=1) * mass_scale
    sums = lax.dot_general(
        weights, rows, (((1,), (0,)), ((), ())), preferred_element_type=jnp.float32
    )
    shifted = centroids.astype(jnp.float32) + sums * mass_scale
    factor = lax.rsqrt(jnp.mean(shifted * shifted, axis=1, keepdims=True) + 1e-06)
    columns = centroids.shape[1] // dp
    own = lax.dynamic_slice_in_dim(shifted, lax.axis_index("dp") * columns, columns, 1)
    return ((own * factor).astype(jnp.bfloat16), loads)


def solution(mesh):
    placed = (P(("dp", "cent"), None), P("cent", None))
    return jax.shard_map(
        on_device,
        mesh=mesh,
        in_specs=placed,
        out_specs=(P("cent", "dp"), P("cent")),
        check_vma=False,
    )
```

profile of v0, /device:TPU:0, one launch (start us, length us, event | category | flops | bytes accessed | tf_op | source)
XLA Modules:
  0.0 130.6 jit_solution(8532630208074017856)
XLA Ops:
  7.2 0.0 all-gather.4.cloned.1.call-start
  7.2 0.7 all-gather.4.cloned.1.call-update
  7.9 11.3 %copy.7 = bf16[4096,1024]{0,1:T(8,128)(2,1)} copy(bf16[4096,1024]{1,0:T(8,128)(2,1)} %param.3) | data formatting | bytes 16777216 | tf_op args[1]
  19.2 48.2 %all-gather.4.cloned.1.call-done = bf16[512,1024]{1,0:T(8,128)(2,1)} async-done(((bf16[16,1024]{1,0:T(8,128)(2,1)}), bf16[512,1024]{1,0:T(8,128)(2,1)}) %all-gather.4.cloned.1.call-update) | async-done | bytes 1048592 | tf_op jit(solution)/shard_map/all_gather | solution.py:14
  67.3 7.4 %multiply_reduce_fusion.2 = (f32[512]{0:T(512)S(1)}, f32[4096,512]{1,0:T(8,128)S(1)}) fusion(bf16[4096,1024]{1,0:T(8,128)(2,1)} %param.3, bf16[512,1024]{1,0:T(8,128)(2,1)} %all-gather.4.cloned.1.call-done), kind=kOutput, calls=%fused_computation.6 | convolution fusion | flops 4299161088 | bytes 17827840 | tf_op jit(solution)/shard_map/dot_general | solution.py:16
  74.8 0.0 copy-start
  74.8 1.5 %fusion = f32[512]{0:T(512)S(1)} fusion(f32[4096,512]{1,0:T(8,128)S(1)} %get-tuple-element.10, f32[512]{0:T(512)S(1)} %get-tuple-element.9), kind=kLoop, calls=%fused_computation.7 | loop fusion | flops 6290944 | bytes 8392704 | tf_op jit(solution)/shard_map/reduce_sum | solution.py:23
  76.2 20.4 %all-gather.1 = f32[16,2,512]{2,1,0:T(2,128)S(1)} all-gather(f32[1,2,512]{2,1,0:T(2,128)S(1)} %maximum_bitcast_fusion), channel_id=2, replica_groups=mesh['dp'=2,'cent'=16] {'cent'}, dimensions={0}, use_global_device_ids=true | all-gather | bytes 69632 | tf_op jit(solution)/shard_map/all_gather | solution.py:24
  96.7 0.1 slice_reduce_fusion
  96.8 1.7 %multiply_reduce_fusion.1 = f32[4096]{0:T(1024)S(1)} fusion(f32[4096,512]{1,0:T(8,128)S(1)} %get-tuple-element.10, f32[512]{0:T(512)S(1)} %exponential_divide_fusion, f32[512]{0:T(512)S(1)} %get-tuple-element.9), kind=kLoop, calls=%fused_computation.4 | loop fusion | flops 8384512 | bytes 8409088 | tf_op jit(solution)/shard_map/reduce_sum | solution.py:30
  98.5 0.0 copy-done
  98.5 11.9 %multiply_reduce_fusion = (f32[4096]{0:T(1024)S(1)}, f32[4096,1024]{0,1:T(8,128)}) fusion(bf16[512,1024]{1,0:T(8,128)(2,1)S(1)} %copy-done, f32[4096,512]{1,0:T(8,128)S(1)} %get-tuple-element.10, f32[512]{0:T(512)S(1)} %exponential_divide_fusion, f32[512]{0:T(512)S(1)} %get-tuple-element.9, bf16[4096,1024]{0,1:T(8,128)(2,1)} %copy.7), kind=kOutput, calls=%fused_computation | convolution fusion | flops 4324323328 | bytes 34623488 | tf_op jit(solution)/shard_map/dot_general | solution.py:31
  110.5 6.3 %multiply_convert_fusion = bf16[4096,512]{0,1:T(8,128)(2,1)} fusion(f32[4096,1024]{0,1:T(8,128)} %get-tuple-element.12, s32[]{:T(128)S(6)} %select_n.3, f32[4096]{0:T(1024)S(1)} %add_rsqrt_fusion), kind=kLoop, calls=%fused_computation.2 | loop fusion | flops 4194304 | bytes 12599300 | tf_op jit(solution)/shard_map/convert_element_type | solution.py:38
  116.7 6.4 %copy.9 = bf16[4096,512]{1,0:T(8,128)(2,1)} copy(bf16[4096,512]{0,1:T(8,128)(2,1)} %multiply_convert_fusion) | data formatting | bytes 8388608
  123.1 0.6 broadcast_multiply_fusion
  (4 shorter events, 0.1 us)
Async XLA Ops:
  7.2 60.2 %all-gather.4.cloned.1.call-start = ((), (), s32[]{:S(2)}) async-start(), calls=%async_computation | async-start | bytes 1081344 | tf_op jit(solution)/shard_map/all_gather | solution.py:14
  74.8 23.8 %copy-start = (bf16[512,1024]{1,0:T(8,128)(2,1)S(1)}, bf16[512,1024]{1,0:T(8,128)(2,1)}, u32[]{:S(2)}) copy-start(bf16[512,1024]{1,0:T(8,128)(2,1)} %all-gather.4.cloned.1.call-done) | copy-start | bytes 3145732
Sparse Core Ops, SparseCore 0:
  10.9 56.4 all-gather.3
where the time goes:
time: 131 us
  waiting for transfers between devices  48.8 us (37%)
  blocking collectives  20.4 us (16%)
  matrix products  19.3 us (15%)
  local copies, waits for them, and re-layouts  17.7 us (14%)
  between operations  14.1 us (11%)
  other arithmetic  10.2 us (8%)
    all_gather x1, waiting for transfers between devices, on_device(): rows = lax.all_gather(vectors, ('dp', 'cent'), axis=0, tiled=True)  48.2 us
    all_gather x1, blocking collectives, on_device(): stats = lax.all_gather(jnp.stack([local_peak, local_sum]), 'cent', axis=0)  20.4 us
    unnamed x4, local copies, waits for them, and re-layouts  17.7 us
    dot_general x1, matrix products, on_device(): lax.dot_general(weights, rows, (((1,), (0,)), ((), ())), preferred_elemen...  11.9 us
    dot_general x1, matrix products, on_device(): lax.dot_general(centroids, rows, (((1,), (1,)), ((), ())), preferred_elem...  7.43 us
    convert_element_type x1, other arithmetic, on_device(): return ((own * factor).astype(jnp.bfloat16), loads)  6.29 us
  transfers between devices with their start and end apart: 1, of which 1 were waited for; matrix products, arithmetic and copies ran while one was open for 9% of the time, Pallas kernels for 0%

commit v1 on v0

--- a/solution.py
+++ b/solution.py
@@ -6,12 +6,35 @@
 softness_scale = 0.1
 
 
+def in_order(parts, dim):
+    shape = list(parts.shape[1:])
+    shape[dim] *= parts.shape[0]
+    return jnp.moveaxis(parts, 0, dim).reshape(shape)
+
+
+def collected_by_bits(x, axis):
+    length, index = (lax.axis_size(axis), lax.axis_index(axis))
+    blocks, bit = (x[None], 1)
+    while bit < length:
+        partner_block = lax.ppermute(blocks, axis, [(i, i ^ bit) for i in range(length)])
+        low = index & bit == 0
+        blocks = jnp.concatenate(
+            [jnp.where(low, blocks, partner_block), jnp.where(low, partner_block, blocks)]
+        )
+        bit *= 2
+    return blocks
+
+
+def doubled_up(shard, axis, dim):
+    return in_order(collected_by_bits(shard, axis), dim)
+
+
 def on_device(vectors, centroids):
     dp = lax.axis_size("dp")
     cent = lax.axis_size("cent")
     total_rows = vectors.shape[0] * dp * cent
     mass_scale = centroids.shape[0] * cent / total_rows
-    rows = lax.all_gather(vectors, ("dp", "cent"), axis=0, tiled=True)
+    rows = doubled_up(vectors, ("dp", "cent"), 0)
     scores = (
         lax.dot_general(
             centroids, rows, (((1,), (1,)), ((), ())), preferred_element_type=jnp.float32

time: 131 us -> 99.2 us (0.76)
  waiting for transfers between devices: 48.8 us -> 18 us
  between operations: 14.1 us -> 0.71 us
  starting transfers between devices: 0.04 us -> 9.22 us
  other arithmetic: 10.2 us -> 13.1 us
    all_gather x1 -> x0, waiting for transfers between devices: 48.2 us -> none  [on_device(): rows = lax.all_gather(vectors, ('dp', 'cent'), axis=0, tiled=True)]
    ppermute x0 -> x5, waiting for transfers between devices: none -> 18 us  [collected_by_bits(): lax.ppermute(blocks, axis, [(i, i ^ bit) for i in range(length)])]
    ppermute x0 -> x5, starting transfers between devices: none -> 9.22 us  [collected_by_bits(): lax.ppermute(blocks, axis, [(i, i ^ bit) for i in range(length)])]
    unnamed x4 -> x8, local copies, waits for them, and re-layouts: 17.7 us -> 18.2 us
  transfers between devices with their start and end apart: 1 -> 5, of which waited for: 1 -> 5; matrix products, arithmetic and copies ran while one was open for 9% -> 12% of each run, Pallas kernels for 0% -> 0%
where the time goes in v1:
time: 99.2 us; the launch traced here: 98.6 us
  blocking collectives  21.3 us (21%)
  local copies, waits for them, and re-layouts  18.2 us (18%)
  waiting for transfers between devices  18 us (18%)
  matrix products  18 us (18%)
  other arithmetic  13.1 us (13%)
  starting transfers between devices  9.22 us (9%)
    all_gather x1, blocking collectives, on_device(): stats = lax.all_gather(jnp.stack([local_peak, local_sum]), 'cent', axis=0)  21.3 us
    unnamed x8, local copies, waits for them, and re-layouts  18.2 us
    ppermute x5, waiting for transfers between devices, collected_by_bits(): lax.ppermute(blocks, axis, [(i, i ^ bit) for i in range(length)])  18 us
    dot_general x1, matrix products, on_device(): lax.dot_general(weights, rows, (((1,), (0,)), ((), ())), preferred_elemen...  10.8 us
    ppermute x5, starting transfers between devices, collected_by_bits(): lax.ppermute(blocks, axis, [(i, i ^ bit) for i in range(length)])  9.22 us
    dot_general x1, matrix products, on_device(): lax.dot_general(centroids, rows, (((1,), (1,)), ((), ())), preferred_elem...  7.13 us
    convert_element_type x1, other arithmetic, on_device(): return ((own * factor).astype(jnp.bfloat16), loads)  6.31 us
    reduce_sum x1, other arithmetic, on_device(): loads = jnp.sum(probability, axis=1) * mass_scale  2.76 us
  transfers between devices with their start and end apart: 5, of which 5 were waited for; matrix products, arithmetic and copies ran while one was open for 12% of the time, Pallas kernels for 0%

profile of v1, /device:TPU:0, one launch (start us, length us, event | category | flops | bytes accessed | tf_op | source)
XLA Modules:
  0.0 98.6 jit_solution(1732982555747620416)
XLA Ops:
  0.6 0.5 collective-permute-start
  1.1 1.1 %collective-permute-done = bf16[1,16,1024]{2,1,0:T(8,128)(2,1)S(1)} collective-permute-done((bf16[1,16,1024]{2,1,0:T(8,128)(2,1)}, bf16[1,16,1024]{2,1,0:T(8,128)(2,1)S(1)}, u32[]{:S(2)}, u32[]{:S(2)}) %collective-permute-start) | collective-permute-done | bytes 32800 | tf_op jit(solution)/shard_map/ppermute | solution.py:19
  2.2 0.8 broadcast_select_fusion.9
  3.0 2.9 %collective-permute-start.1 = (bf16[2,16,1024]{2,1,0:T(8,128)(2,1)S(1)}, bf16[2,16,1024]{2,1,0:T(8,128)(2,1)S(1)}, u32[]{:S(2)}, u32[]{:S(2)}) collective-permute-start(bf16[2,16,1024]{2,1,0:T(8,128)(2,1)S(1)} %pad_maximum_fusion.4), channel_id=1, source_target_pairs={{0,2},{1,3},{2,0},{3,1},{4,6},{5,7},{6,4},{7,5},{8,10},{9,11},{10,... | collective-permute-start | bytes 196616 | tf_op jit(solution)/shard_map/ppermute | solution.py:19
  5.9 2.4 %collective-permute-done.1 = bf16[2,16,1024]{2,1,0:T(8,128)(2,1)S(1)} collective-permute-done((bf16[2,16,1024]{2,1,0:T(8,128)(2,1)S(1)}, bf16[2,16,1024]{2,1,0:T(8,128)(2,1)S(1)}, u32[]{:S(2)}, u32[]{:S(2)}) %collective-permute-start.1) | collective-permute-done | bytes 65568 | tf_op jit(solution)/shard_map/ppermute | solution.py:19
  8.4 2.0 %collective-permute-start.2 = (bf16[4,16,1024]{2,1,0:T(8,128)(2,1)S(1)}, bf16[4,16,1024]{2,1,0:T(8,128)(2,1)S(1)}, u32[]{:S(2)}, u32[]{:S(2)}) collective-permute-start(bf16[4,16,1024]{2,1,0:T(8,128)(2,1)S(1)} %pad_maximum_fusion.3), channel_id=1, source_target_pairs={{0,4},{1,5},{2,6},{3,7},{4,0},{5,1},{6,2},{7,3},{8,12},{9,13},{10,... | collective-permute-start | bytes 393224 | tf_op jit(solution)/shard_map/ppermute | solution.py:19
  10.4 3.1 %collective-permute-done.2 = bf16[4,16,1024]{2,1,0:T(8,128)(2,1)S(1)} collective-permute-done((bf16[4,16,1024]{2,1,0:T(8,128)(2,1)S(1)}, bf16[4,16,1024]{2,1,0:T(8,128)(2,1)S(1)}, u32[]{:S(2)}, u32[]{:S(2)}) %collective-permute-start.2) | collective-permute-done | bytes 131104 | tf_op jit(solution)/shard_map/ppermute | solution.py:19
  13.6 2.9 %collective-permute-start.3 = (bf16[8,16,1024]{2,1,0:T(8,128)(2,1)S(1)}, bf16[8,16,1024]{2,1,0:T(8,128)(2,1)S(1)}, u32[]{:S(2)}, u32[]{:S(2)}) collective-permute-start(bf16[8,16,1024]{2,1,0:T(8,128)(2,1)S(1)} %pad_maximum_fusion.2), channel_id=1, source_target_pairs={{0,8},{1,9},{2,10},{3,11},{4,12},{5,13},{6,14},{7,15},{8,0},{9,1},... | collective-permute-start | bytes 786440 | tf_op jit(solution)/shard_map/ppermute | solution.py:19
  16.5 10.6 %collective-permute-done.3 = bf16[8,16,1024]{2,1,0:T(8,128)(2,1)S(1)} collective-permute-done((bf16[8,16,1024]{2,1,0:T(8,128)(2,1)S(1)}, bf16[8,16,1024]{2,1,0:T(8,128)(2,1)S(1)}, u32[]{:S(2)}, u32[]{:S(2)}) %collective-permute-start.3) | collective-permute-done | bytes 262176 | tf_op jit(solution)/shard_map/ppermute | solution.py:19
  27.2 0.9 collective-permute-start.4
  28.1 11.8 %copy.7 = bf16[4096,1024]{0,1:T(8,128)(2,1)} copy(bf16[4096,1024]{1,0:T(8,128)(2,1)} %param.3) | data formatting | bytes 16777216 | tf_op args[1]
  39.9 0.8 collective-permute-done.4
  40.7 0.1 broadcast_select_fusion.1
  40.8 0.1 pad_maximum_fusion
  40.9 7.1 %multiply_reduce_fusion.2 = (f32[512]{0:T(512)S(1)}, f32[512,4096]{1,0:T(8,128)S(1)}) fusion(bf16[512,1024]{1,0:T(8,128)(2,1)S(1)} %bitcast.25, bf16[4096,1024]{1,0:T(8,128)(2,1)} %param.3), kind=kOutput, calls=%fused_computation.6 | convolution fusion | flops 4299161088 | bytes 17827840 | tf_op jit(solution)/shard_map/dot_general | solution.py:39
  48.0 1.5 %fusion = f32[512]{0:T(512)S(1)} fusion(f32[512,4096]{1,0:T(8,128)S(1)} %get-tuple-element.20, f32[512]{0:T(512)S(1)} %get-tuple-element.19), kind=kLoop, calls=%fused_computation.7 | loop fusion | flops 6290944 | bytes 8392704 | tf_op jit(solution)/shard_map/reduce_sum | solution.py:46
  49.5 21.3 %all-gather.1 = f32[16,2,512]{2,1,0:T(2,128)S(1)} all-gather(f32[1,2,512]{2,1,0:T(2,128)S(1)} %maximum_bitcast_fusion), channel_id=2, replica_groups=mesh['dp'=2,'cent'=16] {'cent'}, dimensions={0}, use_global_device_ids=true | all-gather | bytes 69632 | tf_op jit(solution)/shard_map/all_gather | solution.py:47
  70.8 0.1 slice_reduce_fusion
  70.9 2.8 %multiply_reduce_fusion.1 = f32[4096]{0:T(1024)} fusion(f32[512,4096]{1,0:T(8,128)S(1)} %get-tuple-element.20, f32[512]{0:T(512)S(1)} %exponential_divide_fusion, f32[512]{0:T(512)S(1)} %get-tuple-element.19), kind=kLoop, calls=%fused_computation.4 | loop fusion | flops 8384512 | bytes 8409088 | tf_op jit(solution)/shard_map/reduce_sum | solution.py:53
  73.7 10.8 %multiply_reduce_fusion = (f32[4096]{0:T(1024)}, f32[4096,1024]{0,1:T(8,128)}) fusion(bf16[512,1024]{1,0:T(8,128)(2,1)S(1)} %bitcast.26, f32[512,4096]{1,0:T(8,128)S(1)} %get-tuple-element.20, f32[512]{0:T(512)S(1)} %exponential_divide_fusion, f32[512]{0:T(512)S(1)} %get-tuple-element.19, bf16[4096,1024]{0,1:T(8,128)(2,1)S(1)} %bitcast.24), kind=kOutput, calls=%fused_computation | convolution fusion | flops 4324323328 | bytes 34623488 | tf_op jit(solution)/shard_map/dot_general | solution.py:54
  84.5 0.7 add_rsqrt_fusion
  85.3 6.3 %multiply_convert_fusion = bf16[4096,512]{0,1:T(8,128)(2,1)} fusion(f32[4096,1024]{0,1:T(8,128)} %get-tuple-element.22, s32[]{:T(128)S(6)} %select_n.78, f32[4096]{0:T(1024)S(1)} %add_rsqrt_fusion), kind=kLoop, calls=%fused_computation.2 | loop fusion | flops 4194304 | bytes 12599300 | tf_op jit(solution)/shard_map/convert_element_type | solution.py:61
  91.6 6.4 %copy.9 = bf16[4096,512]{1,0:T(8,128)(2,1)} copy(bf16[4096,512]{0,1:T(8,128)(2,1)} %multiply_convert_fusion) | data formatting | bytes 8388608
  98.0 0.6 broadcast_multiply_fusion
  (17 shorter events, 0.2 us)
Async XLA Ops:
  0.6 1.6 %collective-permute-start = (bf16[1,16,1024]{2,1,0:T(8,128)(2,1)}, bf16[1,16,1024]{2,1,0:T(8,128)(2,1)S(1)}, u32[]{:S(2)}, u32[]{:S(2)}) collective-permute-start(bf16[1,16,1024]{2,1,0:T(8,128)(2,1)} %bitcast.27), channel_id=1, source_target_pairs={{0,1},{1,0},{2,3},{3,2},{4,5},{5,4},{6,7},{7,6},{8,9},{9,8},{10,11... | collective-permute-start | bytes 98312 | tf_op jit(solution)/shard_map/ppermute | solution.py:19
  3.0 5.3 %collective-permute-start.1 = (bf16[2,16,1024]{2,1,0:T(8,128)(2,1)S(1)}, bf16[2,16,1024]{2,1,0:T(8,128)(2,1)S(1)}, u32[]{:S(2)}, u32[]{:S(2)}) collective-permute-start(bf16[2,16,1024]{2,1,0:T(8,128)(2,1)S(1)} %pad_maximum_fusion.4), channel_id=1, source_target_pairs={{0,2},{1,3},{2,0},{3,1},{4,6},{5,7},{6,4},{7,5},{8,10},{9,11},{10,... | collective-permute-start | bytes 196616 | tf_op jit(solution)/shard_map/ppermute | solution.py:19
  8.4 5.1 %collective-permute-start.2 = (bf16[4,16,1024]{2,1,0:T(8,128)(2,1)S(1)}, bf16[4,16,1024]{2,1,0:T(8,128)(2,1)S(1)}, u32[]{:S(2)}, u32[]{:S(2)}) collective-permute-start(bf16[4,16,1024]{2,1,0:T(8,128)(2,1)S(1)} %pad_maximum_fusion.3), channel_id=1, source_target_pairs={{0,4},{1,5},{2,6},{3,7},{4,0},{5,1},{6,2},{7,3},{8,12},{9,13},{10,... | collective-permute-start | bytes 393224 | tf_op jit(solution)/shard_map/ppermute | solution.py:19
  13.6 13.5 %collective-permute-start.3 = (bf16[8,16,1024]{2,1,0:T(8,128)(2,1)S(1)}, bf16[8,16,1024]{2,1,0:T(8,128)(2,1)S(1)}, u32[]{:S(2)}, u32[]{:S(2)}) collective-permute-start(bf16[8,16,1024]{2,1,0:T(8,128)(2,1)S(1)} %pad_maximum_fusion.2), channel_id=1, source_target_pairs={{0,8},{1,9},{2,10},{3,11},{4,12},{5,13},{6,14},{7,15},{8,0},{9,1},... | collective-permute-start | bytes 786440 | tf_op jit(solution)/shard_map/ppermute | solution.py:19
  27.2 13.5 %collective-permute-start.4 = (bf16[16,16,1024]{2,1,0:T(8,128)(2,1)S(1)}, bf16[16,16,1024]{2,1,0:T(8,128)(2,1)S(1)}, u32[]{:S(2)}, u32[]{:S(2)}) collective-permute-start(bf16[16,16,1024]{2,1,0:T(8,128)(2,1)S(1)} %pad_maximum_fusion.1), channel_id=1, source_target_pairs={{0,16},{1,17},{2,18},{3,19},{4,20},{5,21},{6,22},{7,23},{8,24},{9,... | collective-permute-start | bytes 1572872 | tf_op jit(solution)/shard_map/ppermute | solution.py:19
  48.0 25.7 %slice-start = ((s8[8388608]{0:T(1024)(128)(4,1)}), s8[4194304]{0:T(1024)(128)(4,1)S(1)}, s32[]{:S(2)}) async-start(s8[8388608]{0:T(1024)(128)(4,1)} %bitcast.23), calls=%async_computation | async-start | bytes 8388608
  70.8 2.9 %slice-start.1 = ((s8[8388608]{0:T(1024)(128)(4,1)}), s8[4194304]{0:T(1024)(128)(4,1)S(1)}, s32[]{:S(2)}) async-start(s8[8388608]{0:T(1024)(128)(4,1)} %bitcast.23), calls=%async_computation.1 | async-start | bytes 8388608
  85.3 12.7 %copy-start = (f32[4096]{0:T(1024)S(1)}, f32[4096]{0:T(1024)}, u32[]{:S(2)}) copy-start(f32[4096]{0:T(1024)} %multiply_reduce_fusion.1) | copy-start | bytes 49156
